TPU v7x, 128 devices: a whole 4x4x4 slice. The times are simulated.
128 devices in a mesh: row: 16 (over z, x_hi, core), col: 8 (over x_lo, y).
Axes of the slice: x: 4 (x_hi: 2, x_lo: 2; x = x_hi * 2 + x_lo), y: 4, z: 4, core: 2. Of those that a mesh axis runs over, the one named last changes fastest.
Arguments:
- vectors: bfloat16 [256, 64, 128], P(('col', 'row')), may hold values from -6 to 6
- b1_rows: int32 [16, 8, 32], P('row', 'col'), may hold values from 0 to 7, as said below
- b1_cols: int32 [16, 8, 32], P('row', 'col'), may hold values from 0 to 31, as said below
- b1_count: int32 [16, 8], P('row', 'col'), may hold values from 16 to 32, as said below
- b1_values: bfloat16 [16, 8, 32, 128, 128], P('row', 'col'), may hold values from -1 to 1, as said below
- b2_rows: int32 [16, 8, 256], P('row', 'col'), may hold values from 0 to 31, as said below
- b2_cols: int32 [16, 8, 256], P('row', 'col'), may hold values from 0 to 63, as said below
- b2_count: int32 [16, 8], P('row', 'col'), may hold values from 128 to 256, as said below
- b2_values: bfloat16 [16, 8, 256, 128, 128], P('row', 'col'), may hold values from -1 to 1, as said below
Outputs:
- subspace: float32 [256, 64, 128], P(('col', 'row'))
Inputs may be any that keep to these rules, and one draw needn't show every extreme that they name: `b1_rows`: row block within the device's row range; the (row, column) pairs of one device's list are distinct; slots at or past that device's count are ignored. `b1_cols`: unknown block within the device's column range. `b1_count`: one device in every draw uses all 32 slots. `b1_values`: every entry is +1 or -1. `b2_rows`: unknown block within the device's column range; the (row, column) pairs of one device's list are distinct; slots at or past that device's count are ignored. `b2_cols`: column block within the device's row range. `b2_count`: one device in every draw uses all 256 slots. `b2_values`: every entry is +1 or -1.
All inputs are finite; a program needn't handle non-finite values.
Results may differ from a plain program's by a relative error of at most 0.01.
Values may be sent and summed in bfloat16 or wider, within the bound.
A program may use at most 128 MiB of HBM per device.

v0:
```python
import jax
import jax.numpy as jnp
from jax import lax
from jax.sharding import PartitionSpec as P

BLOCK = 128
APPS = 3
EB_DEV = 2
VB_DEV = 1
TB_DEV = 8
NB1 = 32
NB2 = 256


def apply_blocks(values, block_rows, block_cols, filled, source, segments, transpose):
    active = jnp.arange(values.shape[0], dtype=jnp.int32) < filled
    if transpose:
        picked = jnp.take(source, block_rows, axis=0)
        products = jnp.einsum("bji,bkj->bki", values, picked, preferred_element_type=jnp.float32)
        target = block_cols
    else:
        picked = jnp.take(source, block_cols, axis=0)
        products = jnp.einsum("bij,bkj->bki", values, picked, preferred_element_type=jnp.float32)
        target = block_rows
    onehot = (
        (jnp.arange(segments, dtype=jnp.int32)[:, None] == target[None, :]) & active[None, :]
    ).astype(jnp.bfloat16)
    upper = products.astype(jnp.bfloat16)
    lower = (products - upper.astype(jnp.float32)).astype(jnp.bfloat16)
    first = jnp.einsum("sb,bki->ski", onehot, upper, preferred_element_type=jnp.float32)
    second = jnp.einsum("sb,bki->ski", onehot, lower, preferred_element_type=jnp.float32)
    return first + second


def shards(vectors, b1_rows, b1_cols, b1_count, b1_values, b2_rows, b2_cols, b2_count, b2_values):
    vertex_blocks = VB_DEV * lax.axis_size("col")
    triangle_blocks = TB_DEV * lax.axis_size("col")
    inverse_norm = 1.0 / (BLOCK * (NB1 + NB2) // EB_DEV)
    first_rows, first_cols, first_filled, first_values = (
        b1_rows[0, 0],
        b1_cols[0, 0],
        b1_count[0, 0],
        b1_values[0, 0],
    )
    second_rows, second_cols, second_filled, second_values = (
        b2_rows[0, 0],
        b2_cols[0, 0],
        b2_count[0, 0],
        b2_values[0, 0],
    )
    current = vectors
    scaled = vectors.astype(jnp.float32)
    for repeat in range(APPS):
        gathered = lax.all_gather(current, "row", axis=0, tiled=True)
        edge_blocks = gathered.shape[0]
        vertex_part = apply_blocks(
            first_values, first_rows, first_cols, first_filled, gathered, vertex_blocks, False
        )
        triangle_part = apply_blocks(
            second_values, second_rows, second_cols, second_filled, gathered, triangle_blocks, True
        )
        vertex_total, triangle_total = lax.psum((vertex_part, triangle_part), "col")
        vertex_half = vertex_total.astype(jnp.bfloat16)
        triangle_half = triangle_total.astype(jnp.bfloat16)
        edge_from_vertices = apply_blocks(
            first_values, first_rows, first_cols, first_filled, vertex_half, edge_blocks, True
        )
        edge_from_triangles = apply_blocks(
            second_values,
            second_rows,
            second_cols,
            second_filled,
            triangle_half,
            edge_blocks,
            False,
        )
        result = lax.psum_scatter(
            edge_from_vertices + edge_from_triangles, "row", scatter_dimension=0, tiled=True
        )
        scaled = result * inverse_norm
        current = scaled.astype(jnp.bfloat16)
    return scaled


def solution(mesh):
    return jax.shard_map(
        shards,
        mesh=mesh,
        in_specs=(
            P(("col", "row"), None, None),
            P("row", "col", None),
            P("row", "col", None),
            P("row", "col"),
            P("row", "col", None, None, None),
            P("row", "col", None),
            P("row", "col", None),
            P("row", "col"),
            P("row", "col", None, None, None),
        ),
        out_specs=P(("col", "row"), None, None),
        check_vma=False,
    )
```

profile of v0, /device:TPU:0, one launch (start us, length us, event | category | flops | bytes accessed | tf_op | source)
XLA Modules:
  0.0 657.7 jit_solution(8362919779539080046)
XLA Ops:
  13.6 28.1 %all_gather.9 = bf16[32,64,128]{2,1,0:T(8,128)(2,1)S(1)} all-gather(bf16[2,64,128]{2,1,0:T(8,128)(2,1)} %param.17), channel_id=1, replica_groups=mesh['row'=16,'col'=8] {'row'}, dimensions={0}, use_global_device_ids=true | all-gather | bytes 557056 | tf_op jit(solution)/shard_map/all_gather | solution.py:54
  42.3 3.1 gather_fusion.2
  45.4 7.1 %subtract_convert_fusion.5 = (bf16[256,64,128]{2,1,0:T(8,128)(2,1)S(1)}, bf16[256,64,128]{2,1,0:T(8,128)(2,1)S(1)}) fusion(bf16[1,1,256,128,128]{4,3,2,1,0:T(8,128)(2,1)} %param.25, bf16[256,64,128]{2,1,0:T(8,128)(2,1)} %gather_fusion.2, pred[256]{0:T(512)(128)(4,1)S(1)} %compare_and_fusion.3), kind=kOutput, calls=%fused_computation.29 | convolution fusion | flops 547356672 | bytes 20971776 | tf_op jit(solution)/shard_map/bji,bkj->bki/dot_general | solution.py:19
  52.4 2.5 fusion.32
  55.0 4.0 fusion.54
  64.0 74.3 %all-reduce.6 = (bf16[64,64,128]{2,0,1:T(8,128)(2,1)}, bf16[8,64,128]{2,0,1:T(8,128)(2,1)S(1)}) all-reduce(f32[64,64,128]{2,0,1:T(8,128)S(1)} %copy-done.6, f32[8,64,128]{2,0,1:T(8,128)S(1)} %convolution_add_fusion.5), channel_id=1, replica_groups=mesh['row'=16,'col'=8] {'col'}, use_global_device_ids=true, to_apply=%region_1.0 | all-reduce | flops 589824 | bytes 3538944 | tf_op jit(solution)/shard_map/psum | solution.py:62
  140.2 3.1 gather_fusion.3
  143.3 13.6 %subtract_convert_fusion.4 = (bf16[256,64,128]{2,1,0:T(8,128)(2,1)}, bf16[256,64,128]{2,1,0:T(8,128)(2,1)}) fusion(bf16[1,1,256,128,128]{4,3,2,1,0:T(8,128)(2,1)} %param.25, bf16[256,64,128]{2,1,0:T(8,128)(2,1)} %gather_fusion.3, pred[256]{0:T(512)(128)(4,1)S(1)} %copy-done.19), kind=kOutput, calls=%fused_computation.28 | convolution fusion | flops 547356672 | bytes 20971776 | tf_op jit(solution)/shard_map/bij,bkj->bki/dot_general | solution.py:23
  157.0 4.8 fusion.28
  168.0 61.8 %reduce-scatter.4.cloned.1.call-done = f32[2,64,128]{2,1,0:T(8,128)} async-done(((f32[32,64,128]{2,1,0:T(8,128)}), f32[2,64,128]{2,1,0:T(8,128)}) %reduce-scatter.4.cloned.1.call-update) | async-done | bytes 65552 | tf_op jit(solution)/shard_map/reduce_scatter | solution.py:77
  230.6 24.2 %all_gather.10 = bf16[32,64,128]{2,1,0:T(8,128)(2,1)S(1)} all-gather(bf16[2,64,128]{2,1,0:T(8,128)(2,1)S(1)} %multiply_convert_fusion.1), channel_id=1, replica_groups=mesh['row'=16,'col'=8] {'row'}, dimensions={0}, use_global_device_ids=true | all-gather | bytes 557056 | tf_op jit(solution)/shard_map/all_gather | solution.py:54
  255.6 3.3 gather_fusion.6
  261.2 5.8 subtract_convert_fusion.3
  267.0 2.5 fusion.24
  269.5 2.7 fusion.57
  272.2 74.7 %all-reduce.7 = (bf16[64,64,128]{2,0,1:T(8,128)(2,1)}, bf16[8,64,128]{2,0,1:T(8,128)(2,1)S(1)}) all-reduce(f32[64,64,128]{2,0,1:T(8,128)S(1)} %fusion.57, f32[8,64,128]{2,0,1:T(8,128)S(1)} %convolution_add_fusion.4), channel_id=1, replica_groups=mesh['row'=16,'col'=8] {'col'}, use_global_device_ids=true, to_apply=%region_4.0 | all-reduce | flops 589824 | bytes 3538944 | tf_op jit(solution)/shard_map/psum | solution.py:62
  348.8 3.2 gather_fusion.7
  352.0 13.7 %subtract_convert_fusion.2 = (bf16[256,64,128]{2,1,0:T(8,128)(2,1)}, bf16[256,64,128]{2,1,0:T(8,128)(2,1)}) fusion(bf16[1,1,256,128,128]{4,3,2,1,0:T(8,128)(2,1)} %param.25, bf16[256,64,128]{2,1,0:T(8,128)(2,1)} %gather_fusion.7, pred[256]{0:T(512)(128)(4,1)S(1)} %copy-done.20), kind=kOutput, calls=%fused_computation.26 | convolution fusion | flops 547356672 | bytes 20971776 | tf_op jit(solution)/shard_map/bij,bkj->bki/dot_general | solution.py:23
  365.7 4.6 fusion.20
  373.3 2.5 fusion.66
  377.9 61.8 %reduce-scatter.6.cloned.1.call-done = f32[2,64,128]{2,1,0:T(8,128)} async-done(((f32[32,64,128]{2,1,0:T(8,128)}), f32[2,64,128]{2,1,0:T(8,128)}) %reduce-scatter.6.cloned.1.call-update) | async-done | bytes 65552 | tf_op jit(solution)/shard_map/reduce_scatter | solution.py:77
  440.5 24.0 %all_gather.11 = bf16[32,64,128]{2,1,0:T(8,128)(2,1)S(1)} all-gather(bf16[2,64,128]{2,1,0:T(8,128)(2,1)S(1)} %multiply_convert_fusion), channel_id=1, replica_groups=mesh['row'=16,'col'=8] {'row'}, dimensions={0}, use_global_device_ids=true | all-gather | bytes 557056 | tf_op jit(solution)/shard_map/all_gather | solution.py:54
  465.3 3.3 gather_fusion.10
  470.9 5.8 subtract_convert_fusion.1
  476.7 2.5 fusion.16
  479.2 2.7 fusion.60
  481.9 74.6 %all-reduce.8 = (bf16[64,64,128]{2,0,1:T(8,128)(2,1)}, bf16[8,64,128]{2,0,1:T(8,128)(2,1)S(1)}) all-reduce(f32[64,64,128]{2,0,1:T(8,128)S(1)} %fusion.60, f32[8,64,128]{2,0,1:T(8,128)S(1)} %convolution_add_fusion.3), channel_id=1, replica_groups=mesh['row'=16,'col'=8] {'col'}, use_global_device_ids=true, to_apply=%region_7.12 | all-reduce | flops 589824 | bytes 3538944 | tf_op jit(solution)/shard_map/psum | solution.py:62
  558.4 3.2 gather_fusion.11
  561.6 13.6 %subtract_convert_fusion = (bf16[256,64,128]{2,1,0:T(8,128)(2,1)}, bf16[256,64,128]{2,1,0:T(8,128)(2,1)}) fusion(bf16[1,1,256,128,128]{4,3,2,1,0:T(8,128)(2,1)} %param.25, bf16[256,64,128]{2,1,0:T(8,128)(2,1)} %gather_fusion.11, pred[256]{0:T(512)(128)(4,1)S(1)} %copy-done.21), kind=kOutput, calls=%fused_computation.24 | convolution fusion | flops 547356672 | bytes 20971776 | tf_op jit(solution)/shard_map/bij,bkj->bki/dot_general | solution.py:23
  575.3 4.6 fusion.12
  582.9 2.5 fusion.69
  587.4 61.9 %reduce-scatter.8.cloned.1.call-done = f32[2,64,128]{2,1,0:T(8,128)} async-done(((f32[32,64,128]{2,1,0:T(8,128)}), f32[2,64,128]{2,1,0:T(8,128)}) %reduce-scatter.8.cloned.1.call-update) | async-done | bytes 65552 | tf_op jit(solution)/shard_map/reduce_scatter | solution.py:77
  (121 shorter events, 42.2 us)
Async XLA Ops:
  6.5 54.6 %copy-start = (bf16[1,1,32,128,128]{4,3,2,1,0:T(8,128)(2,1)S(1)}, bf16[1,1,32,128,128]{4,3,2,1,0:T(8,128)(2,1)}, u32[]{:S(2)}) copy-start(bf16[1,1,32,128,128]{4,3,2,1,0:T(8,128)(2,1)} %param.21) | copy-start | bytes 3145732
  6.5 223.2 %reduce-scatter.4.cloned.1.call-start = ((), (), s32[]{:S(2)}) async-start(), calls=%async_computation.3 | async-start | bytes 1114112 | tf_op jit(solution)/shard_map/reduce_scatter | solution.py:77
  8.0 37.4 %copy-start.22 = (pred[256]{0:T(512)(128)(4,1)}, pred[256]{0:T(512)(128)(4,1)S(1)}, u32[]{:S(2)}) copy-start(pred[256]{0:T(512)(128)(4,1)S(1)} %compare_and_fusion.3) | copy-start | bytes 772
  9.3 51.8 %copy-start.28 = (pred[32]{0:T(512)(128)(4,1)}, pred[32]{0:T(512)(128)(4,1)S(1)}, u32[]{:S(2)}) copy-start(pred[32]{0:T(512)(128)(4,1)S(1)} %compare_and_fusion.1) | copy-start | bytes 100
  13.6 31.8 %copy-start.15 = (s32[1024]{0:T(1024)}, s32[1024]{0:T(1024)S(1)}, u32[]{:S(2)}) copy-start(s32[1024]{0:T(1024)S(1)} %pad_clamp_fusion.1) | copy-start | bytes 12292
  45.4 7.1 %copy-start.7 = (s32[1,1,256]{2,1,0:T(1,128)S(1)}, s32[1,1,256]{2,1,0:T(1,128)}, u32[]{:S(2)}) copy-start(s32[1,1,256]{2,1,0:T(1,128)} %param.23) | copy-start | bytes 3076
  55.0 8.2 %copy-start.9 = (s32[1,1,32]{2,1,0:T(1,128)S(1)}, s32[1,1,32]{2,1,0:T(1,128)}, u32[]{:S(2)}) copy-start(s32[1,1,32]{2,1,0:T(1,128)} %param.18) | copy-start | bytes 388
  59.7 3.9 copy-start.18
  61.1 2.8 copy-start.6
  140.2 3.1 copy-start.16
  140.2 3.1 copy-start.19
  143.3 13.6 %copy-start.8 = (s32[1,1,256]{2,1,0:T(1,128)S(1)}, s32[1,1,256]{2,1,0:T(1,128)}, u32[]{:S(2)}) copy-start(s32[1,1,256]{2,1,0:T(1,128)} %param.22) | copy-start | bytes 3076
  157.0 4.8 copy-start.31
  157.0 4.9 copy-start.5
  161.7 3.2 copy-start.25
  161.8 3.6 copy-start.17
  161.8 3.6 copy-start.12
  167.9 271.7 %reduce-scatter.6.cloned.1.call-start = ((), (), s32[]{:S(2)}) async-start(), calls=%async_computation.4 | async-start | bytes 1114112 | tf_op jit(solution)/shard_map/reduce_scatter | solution.py:77
  255.6 3.4 copy-start.29
  255.6 4.2 copy-start.10
  259.0 2.2 copy-start.23
  348.8 3.2 copy-start.20
  365.7 5.4 copy-start.26
  365.7 5.9 copy-start.13
  371.1 2.2 copy-start.3
  377.8 271.5 %reduce-scatter.8.cloned.1.call-start = ((), (), s32[]{:S(2)}) async-start(), calls=%async_computation.5 | async-start | bytes 1114112 | tf_op jit(solution)/shard_map/reduce_scatter | solution.py:77
  465.3 3.4 copy-start.30
  465.3 4.2 copy-start.11
  468.7 2.2 copy-start.24
  558.4 3.2 copy-start.21
  575.3 5.4 copy-start.27
  575.3 5.9 copy-start.14
  (3 other events, 6.6 us)
Sparse Core Ops, SparseCore 0:
  168.0 61.6 reduce-scatter.3
  377.9 61.6 reduce-scatter.5
  587.6 61.7 reduce-scatter.7
where the time goes:
time: 666 us; the launch traced here: 658 us
  blocking collectives  300 us (45%)
  waiting for transfers between devices  185 us (28%)
  matrix products  108 us (16%)
  local copies, waits for them, and re-layouts  38.7 us (6%)
  between operations  15.3 us (2%)
  other arithmetic  10.2 us (2%)
    psum x3, blocking collectives, shards(): vertex_total, triangle_total = lax.psum((vertex_part, triangle_part), 'col')  224 us
    reduce_scatter x3, waiting for transfers between devices, shards(): lax.psum_scatter(edge_from_vertices + edge_from_triangles, 'row', scatter...  185 us
    all_gather x3, blocking collectives, shards(): gathered = lax.all_gather(current, 'row', axis=0, tiled=True)  76.3 us
    dot_general x6, matrix products, apply_blocks(): jnp.einsum('bij,bkj->bki', values, picked, preferred_element_type=jnp.flo...  44.6 us
    dot_general x12, matrix products, apply_blocks(): jnp.einsum('sb,bki->ski', onehot, lower, preferred_element_type=jnp.float32)  24.1 us
    dot_general x6, matrix products, apply_blocks(): jnp.einsum('bji,bkj->bki', values, picked, preferred_element_type=jnp.flo...  20.1 us
    dot_general x12, matrix products, apply_blocks(): jnp.einsum('sb,bki->ski', onehot, upper, preferred_element_type=jnp.float32)  19.3 us
  transfers between devices with their start and end apart: 3, of which 3 were waited for; matrix products, arithmetic and copies ran while one was open for 0% of the time, Pallas kernels for 0%

commit v1 on v0

v1 whole, which is shorter than its diff:
```python
import functools

import jax
import jax.numpy as jnp
from jax import lax
from jax.experimental import pallas as pl
from jax.experimental.pallas import tpu as pltpu
from jax.sharding import PartitionSpec as P

BLOCK = 128
K = 64
APPS = 3
NB1 = 32
NB2 = 256
VB_ROW = 8
TB_ROW = 64
EB_COL = 32
NORM = 18432
N_ROW = 16
N_COL = 8
OWN = EB_COL // N_ROW
FACES = 1 + TB_ROW // N_COL
UNROLL = 8
MESH = pl.DeviceIdType.MESH
F32 = jnp.float32
BF16 = jnp.bfloat16

FC, FA, BC, BA = range(4)


def plan_kernel(counts, b1_rows, b1_cols, b2_rows, b2_cols, ints, floats):
    def plan(which, target, source, filled, segments):
        n = target.shape[1]
        lanes = lax.broadcasted_iota(jnp.int32, (n, n), 1)
        rows = lax.broadcasted_iota(jnp.int32, (n, n), 0)
        place = lax.broadcasted_iota(jnp.int32, (1, n), 1)
        target = jnp.where(place < filled, target, segments)
        key = target * n + place

        def column(line):
            return jnp.sum(jnp.where(rows == lanes, line, 0), axis=1, keepdims=True)

        rank = jnp.sum(jnp.where(key < column(key), 1, 0), axis=1, keepdims=True)
        hit = rank == lanes
        follows = (rank + 1) == lanes

        def ordered(line, mask):
            return jnp.sum(jnp.where(mask, column(line), 0), axis=0, keepdims=True)

        here = ordered(target, hit)
        before = ordered(target + 1, follows) - 1
        slots = jnp.where(rank >= 0, rows, 0)
        ints[3 * which : 3 * which + 1, :n] = jnp.sum(jnp.where(hit, slots, 0), axis=0, keepdims=True)
        ints[3 * which + 1 : 3 * which + 2, :n] = ordered(source, hit)
        floats[2 * which : 2 * which + 1, :n] = jnp.where(here == before, 1.0, 0.0)
        wide = 128
        segment = lax.broadcasted_iota(jnp.int32, (n, wide), 1)
        upright = column(target)
        end = jnp.sum(jnp.where(upright <= segment, 1, 0), axis=0, keepdims=True)
        start = jnp.sum(jnp.where(upright < segment, 1, 0), axis=0, keepdims=True)
        ints[3 * which + 2 : 3 * which + 3, :wide] = jnp.maximum(end - 1, 0)
        floats[2 * which + 1 : 2 * which + 2, :wide] = jnp.where(end > start, 1.0, 0.0)

    ints[...] = jnp.zeros_like(ints)
    floats[...] = jnp.zeros_like(floats)
    rows1, cols1, rows2, cols2 = b1_rows[...], b1_cols[...], b2_rows[...], b2_cols[...]
    per = TB_ROW // N_COL
    plan(FC, cols2, rows2, counts[1], TB_ROW)
    plan(FA, rows1, cols1, counts[0], VB_ROW)
    plan(BC, rows2, (cols2 // per) * FACES + 1 + cols2 % per, counts[1], EB_COL)
    plan(BA, cols1, rows1 * FACES, counts[0], EB_COL)


def make_plans(counts, b1_rows, b1_cols, b2_rows, b2_cols):
    return pl.pallas_call(
        plan_kernel,
        out_shape=(
            jax.ShapeDtypeStruct((12, NB2), jnp.int32),
            jax.ShapeDtypeStruct((8, NB2), F32),
        ),
        in_specs=[pl.BlockSpec(memory_space=pltpu.SMEM)] + [pl.BlockSpec(memory_space=pltpu.VMEM)] * 4,
        out_specs=(pl.BlockSpec(memory_space=pltpu.VMEM),) * 2,
    )(counts, b1_rows, b1_cols, b2_rows, b2_cols)


def main_kernel(
    apps, compute, comm,
    ints, floats, vectors, b1_hbm, b2_hbm, out,
    b1, b2, x, sums_c, sums_a, part, part_in, faces, image, image_in,
    load_sem, g_send, g_recv, s_send, s_recv, a_send, a_recv, r_send, r_recv,
):
    row, col = lax.axis_index("row"), lax.axis_index("col")
    load1 = pltpu.make_async_copy(b1_hbm, b1, load_sem.at[0])
    load2 = pltpu.make_async_copy(b2_hbm, b2, load_sem.at[1])
    load1.start()
    load2.start()
    row_peers = [lax.rem(row + d, N_ROW) for d in range(1, N_ROW)]
    col_peers = [lax.rem(col + d, N_COL) for d in range(1, N_COL)]

    barrier = pltpu.get_barrier_semaphore()
    for peer in row_peers:
        pl.semaphore_signal(barrier, inc=1, device_id=(peer, col), device_id_type=MESH)
    for peer in col_peers:
        pl.semaphore_signal(barrier, inc=1, device_id=(row, peer), device_id_type=MESH)
    x[pl.ds(OWN * row, OWN)] = vectors[...]
    pl.semaphore_wait(barrier, N_ROW + N_COL - 2)

    def remote(src, dst, sends, recvs, at, device):
        return pltpu.make_async_remote_copy(
            src_ref=src, dst_ref=dst, send_sem=sends.at[at], recv_sem=recvs.at[at],
            device_id=device, device_id_type=MESH,
        )

    def exchange(copies):
        if not comm:
            return
        for copy in copies:
            copy.start()
        for copy in copies:
            copy.wait()

    def sweep(which, n, values, source, sums, turned):
        dims = (((1,), (1,)), ((), ())) if turned else (((1,), (0,)), ((), ()))

        def body(step, total):
            for u in range(UNROLL):
                at = step * UNROLL + u
                product = lax.dot_general(
                    source[ints[3 * which + 1, at]], values[ints[3 * which, at]], dims,
                    preferred_element_type=F32,
                )
                total = total * floats[2 * which, at] + product
                sums[at] = total
            return total

        if compute:
            lax.fori_loop(0, n // UNROLL, body, jnp.zeros((K, BLOCK), F32))

    def picked(which, sums, target):
        return sums[ints[3 * which + 2, target]] * floats[2 * which + 1, target]

    for app in range(apps):
        own = pl.ds(OWN * row, OWN)
        exchange([
            remote(x.at[own], x.at[own], g_send, g_recv, d, (peer, col))
            for d, peer in enumerate(row_peers)
        ])
        if app == 0:
            load1.wait()
            load2.wait()
        sweep(FA, NB1, b1, x, sums_a, True)
        sweep(FC, NB2, b2, x, sums_c, False)

        def hand_faces(m, carry):
            part[m, 0] = picked(FA, sums_a, m).astype(BF16)
            for b in range(FACES - 1):
                part[m, 1 + b] = picked(FC, sums_c, m * (FACES - 1) + b).astype(BF16)
            return carry

        if compute:
            lax.fori_loop(0, N_COL, hand_faces, 0)
        exchange([
            remote(part.at[peer], part_in.at[d], s_send, s_recv, d, (row, peer))
            for d, peer in enumerate(col_peers)
        ])

        def sum_faces(b, carry):
            total = part[col, b].astype(F32)
            for d in range(N_COL - 1):
                total = total + part_in[d, b].astype(F32)
            faces[col * FACES + b] = total.astype(BF16)
            return carry

        if compute:
            lax.fori_loop(0, FACES, sum_faces, 0)
        mine = pl.ds(FACES * col, FACES)
        exchange([
            remote(faces.at[mine], faces.at[mine], a_send, a_recv, d, (row, peer))
            for d, peer in enumerate(col_peers)
        ])
        sweep(BA, NB1, b1, faces, sums_a, False)
        sweep(BC, NB2, b2, faces, sums_c, True)

        def hand_image(m, carry):
            for b in range(OWN):
                t = m * OWN + b
                image[m, b] = (picked(BA, sums_a, t) + picked(BC, sums_c, t)).astype(BF16)
            return carry

        if compute:
            lax.fori_loop(0, N_ROW, hand_image, 0)
        exchange([
            remote(image.at[peer], image_in.at[d], r_send, r_recv, d, (peer, col))
            for d, peer in enumerate(row_peers)
        ])
        for b in range(OWN):
            total = image[row, b].astype(F32)
            for d in range(N_ROW - 1):
                total = total + image_in[d, b].astype(F32)
            total = total * (1.0 / NORM)
            if app == apps - 1:
                out[b] = total
            else:
                x[OWN * row + b] = total.astype(BF16)


def build(mesh, apps=APPS, compute=True, comm=True):
    def shards(vectors, b1_rows, b1_cols, b1_count, b1_values, b2_rows, b2_cols, b2_count, b2_values):
        counts = jnp.concatenate([b1_count[0], b2_count[0]])
        ints, floats = make_plans(counts, b1_rows[0], b1_cols[0], b2_rows[0], b2_cols[0])
        vmem = pl.BlockSpec(memory_space=pltpu.VMEM)
        smem = pl.BlockSpec(memory_space=pltpu.SMEM)
        hbm = pl.BlockSpec(memory_space=pl.ANY)
        dma = pltpu.SemaphoreType.DMA
        return pl.pallas_call(
            functools.partial(main_kernel, apps, compute, comm),
            out_shape=jax.ShapeDtypeStruct((OWN, K, BLOCK), F32),
            in_specs=[smem, smem, vmem, hbm, hbm],
            out_specs=vmem,
            scratch_shapes=[
                pltpu.VMEM((NB1, BLOCK, BLOCK), BF16),
                pltpu.VMEM((NB2, BLOCK, BLOCK), BF16),
                pltpu.VMEM((EB_COL, K, BLOCK), BF16),
                pltpu.VMEM((NB2, K, BLOCK), F32),
                pltpu.VMEM((NB1, K, BLOCK), F32),
                pltpu.VMEM((N_COL, FACES, K, BLOCK), BF16),
                pltpu.VMEM((N_COL - 1, FACES, K, BLOCK), BF16),
                pltpu.VMEM((N_COL * FACES, K, BLOCK), BF16),
                pltpu.VMEM((N_ROW, OWN, K, BLOCK), BF16),
                pltpu.VMEM((N_ROW - 1, OWN, K, BLOCK), BF16),
                dma((2,)),
                dma((N_ROW - 1,)), dma((N_ROW - 1,)),
                dma((N_COL - 1,)), dma((N_COL - 1,)),
                dma((N_COL - 1,)), dma((N_COL - 1,)),
                dma((N_ROW - 1,)), dma((N_ROW - 1,)),
            ],
            compiler_params=pltpu.CompilerParams(
                collective_id=0, has_side_effects=True, vmem_limit_bytes=48 * 2**20
            ),
        )(ints, floats, vectors, b1_values[0, 0], b2_values[0, 0])

    return jax.shard_map(
        shards,
        mesh=mesh,
        in_specs=(
            P(("col", "row"), None, None),
            P("row", "col", None),
            P("row", "col", None),
            P("row", "col"),
            P("row", "col", None, None, None),
            P("row", "col", None),
            P("row", "col", None),
            P("row", "col"),
            P("row", "col", None, None, None),
        ),
        out_specs=P(("col", "row"), None, None),
        check_vma=False,
    )


def solution(mesh):
    return build(mesh)
```

time: 666 us -> 226 us (0.34); the launches traced: 658 us -> 224 us
  blocking collectives: 300 us -> 0 us
  Pallas kernels: 0 us -> 219 us
  waiting for transfers between devices: 185 us -> 0 us
  matrix products: 108 us -> 0 us
  local copies, waits for them, and re-layouts: 38.7 us -> 4.03 us
  between operations: 15.3 us -> 1.31 us
  other arithmetic: 10.2 us -> 0.58 us
    psum x3 -> x0, blocking collectives: 224 us -> none  [shards(): vertex_total, triangle_total = lax.psum((vertex_part, triangle_part), 'col')]
    pallas_call x0 -> x2, Pallas kernels: none -> 219 us  [the longest x1 216 us: shards(): pl.pallas_call(functools.partial(main_kernel, apps, compute, comm), out_s...]
    reduce_scatter x3 -> x0, waiting for transfers between devices: 185 us -> none  [shards(): lax.psum_scatter(edge_from_vertices + edge_from_triangles, 'row', scatter...]
    dot_general x36 -> x0, matrix products: 108 us -> none  [the longest x6 44.6 us: apply_blocks(): jnp.einsum('bij,bkj->bki', values, picked, preferred_element_type=jnp.flo...]
    all_gather x3 -> x0, blocking collectives: 76.3 us -> none  [shards(): gathered = lax.all_gather(current, 'row', axis=0, tiled=True)]
    gather x12 -> x0, local copies, waits for them, and re-layouts: 24.4 us -> none  [the longest x6 12.5 us: apply_blocks(): picked = jnp.take(source, block_cols, axis=0)]
  transfers between devices with their start and end apart: 3 -> 0, of which waited for: 3 -> 0; matrix products, arithmetic and copies ran while one was open for 0% -> 0% of each run, Pallas kernels for 0% -> 0%
where the time goes in v1:
time: 226 us; the launch traced here: 224 us
  Pallas kernels  219 us (97%)
  local copies, waits for them, and re-layouts  4.03 us (2%)
    pallas_call x1, Pallas kernels, shards(): pl.pallas_call(functools.partial(main_kernel, apps, compute, comm), out_s...  216 us

profile of v1, /device:TPU:0, one launch (start us, length us, event | category | flops | bytes accessed | tf_op | source)
XLA Modules:
  0.0 224.4 jit_solution(9121743235273061792)
XLA Ops:
  1.3 0.6 pad_add_fusion.counts
  1.9 2.5 %shard_map.91 = (s32[12,256]{1,0:T(8,128)}, f32[8,256]{1,0:T(8,128)}) custom-call(s32[2]{0:T(128)} %pad_add_fusion.counts, s32[1,32]{1,0:T(1,128)} %bitcast.14, s32[1,32]{1,0:T(1,128)} %bitcast.15, s32[1,256]{1,0:T(1,128)} %bitcast.12, s32[1,256]{1,0:T(1,128)} %bitcast.13), custom_call_target="tpu_custom_call" | custom-call | tf_op jit(solution)/shard_map/pallas_call | solution.py:75
  4.3 0.0 copy-start
  4.4 1.2 copy-done
  5.6 0.0 copy-start.1
  5.6 0.8 copy-done.1
  6.3 0.0 copy-start.2
  6.3 0.7 copy-done.2
  7.1 0.0 copy-start.3
  7.1 0.7 copy-done.3
  7.7 216.0 %shard_map.92 = f32[2,64,128]{2,1,0:T(8,128)S(1)} custom-call(s32[12,256]{1,0:T(8,128)S(1)} %copy-done.2, f32[8,256]{1,0:T(8,128)S(1)} %copy-done.3, bf16[2,64,128]{2,1,0:T(8,128)(2,1)S(1)} %copy-done.1, bf16[32,128,128]{2,1,0:T(8,128)(2,1)S(1)} %bitcast.10, bf16[256,128,128]{2,1,0:T(8,128)(2,1)} %bitcast.11), custom_call_target="tpu_custom_call" | custom-call | tf_op jit(solution)/shard_map/pallas_call | solution.py:215
  223.8 0.6 copy.13
Async XLA Ops:
  4.3 1.2 copy-start
  5.6 0.8 copy-start.1
  6.3 0.7 copy-start.2
  7.1 0.7 copy-start.3

commit v2 on v1

v2 whole, which is shorter than its diff:
```python
import functools

import jax
import jax.numpy as jnp
from jax import lax
from jax.experimental import pallas as pl
from jax.experimental.pallas import tpu as pltpu
from jax.sharding import PartitionSpec as P

BLOCK = 128
K = 64
APPS = 3
NB1 = 32
NB2 = 256
VB_ROW = 8
TB_ROW = 64
EB_COL = 32
NORM = 18432
N_ROW = 16
N_COL = 8
OWN = EB_COL // N_ROW
FACES = 1 + TB_ROW // N_COL
UNROLL = 32
MESH = pl.DeviceIdType.MESH
F32 = jnp.float32
BF16 = jnp.bfloat16

FC, FA, BC, BA = range(4)


def plan_kernel(counts, b1_rows, b1_cols, b2_rows, b2_cols, ints, floats):
    def plan(which, target, source, filled, segments):
        n = target.shape[1]
        lanes = lax.broadcasted_iota(jnp.int32, (n, n), 1)
        rows = lax.broadcasted_iota(jnp.int32, (n, n), 0)
        place = lax.broadcasted_iota(jnp.int32, (1, n), 1)
        target = jnp.where(place < filled, target, segments)
        key = target * n + place

        def column(line):
            return jnp.sum(jnp.where(rows == lanes, line, 0), axis=1, keepdims=True)

        rank = jnp.sum(jnp.where(key < column(key), 1, 0), axis=1, keepdims=True)
        hit = rank == lanes
        follows = (rank + 1) == lanes

        def ordered(line, mask):
            return jnp.sum(jnp.where(mask, column(line), 0), axis=0, keepdims=True)

        here = ordered(target, hit)
        before = ordered(target + 1, follows) - 1
        slots = jnp.where(rank >= 0, rows, 0)
        ints[3 * which : 3 * which + 1, :n] = jnp.sum(jnp.where(hit, slots, 0), axis=0, keepdims=True)
        ints[3 * which + 1 : 3 * which + 2, :n] = ordered(source, hit)
        floats[2 * which : 2 * which + 1, :n] = jnp.where(here == before, 1.0, 0.0)
        wide = 128
        segment = lax.broadcasted_iota(jnp.int32, (n, wide), 1)
        upright = column(target)
        end = jnp.sum(jnp.where(upright <= segment, 1, 0), axis=0, keepdims=True)
        start = jnp.sum(jnp.where(upright < segment, 1, 0), axis=0, keepdims=True)
        ints[3 * which + 2 : 3 * which + 3, :wide] = jnp.maximum(end - 1, 0)
        floats[2 * which + 1 : 2 * which + 2, :wide] = jnp.where(end > start, 1.0, 0.0)

    ints[...] = jnp.zeros_like(ints)
    floats[...] = jnp.zeros_like(floats)
    rows1, cols1, rows2, cols2 = b1_rows[...], b1_cols[...], b2_rows[...], b2_cols[...]
    per = TB_ROW // N_COL
    plan(FC, cols2, rows2, counts[1], TB_ROW)
    plan(FA, rows1, cols1, counts[0], VB_ROW)
    plan(BC, rows2, (cols2 // per) * FACES + 1 + cols2 % per, counts[1], EB_COL)
    plan(BA, cols1, rows1 * FACES, counts[0], EB_COL)


def make_plans(counts, b1_rows, b1_cols, b2_rows, b2_cols):
    return pl.pallas_call(
        plan_kernel,
        out_shape=(
            jax.ShapeDtypeStruct((12, NB2), jnp.int32),
            jax.ShapeDtypeStruct((8, NB2), F32),
        ),
        in_specs=[pl.BlockSpec(memory_space=pltpu.SMEM)] + [pl.BlockSpec(memory_space=pltpu.VMEM)] * 4,
        out_specs=(pl.BlockSpec(memory_space=pltpu.VMEM),) * 2,
    )(counts, b1_rows, b1_cols, b2_rows, b2_cols)


def order_of(apps, parts):
    if parts == 1:
        return [(step, app, 0) for app in range(apps) for step in "YFSBQR"]
    order = []
    for app in range(apps):
        order.append(("Y", app, 0))
        if app:
            order.append(("R", app - 1, 1))
        order += [(step, app, h) for step, h in zip("FYFSSBQBRQ", (0, 1, 1, 0, 1, 0, 0, 1, 0, 1))]
    return order + [("R", apps - 1, 1)]


def main_kernel(
    apps, parts, compute, order,
    ints, floats, vectors, b1_hbm, b2_hbm, out,
    b1, b2, b1_turned, b2_turned, x, sums_c, sums_a, part, part_in, faces,
    kept, lent, lent_in, middle, middle_in,
    load_sem, g_send, g_recv, y_send, y_recv, s_send, s_recv, a_send, a_recv, q_send, q_recv, r_send, r_recv,
):
    row, col = lax.axis_index("row"), lax.axis_index("col")
    height = K // parts
    chip, core = row // 2, lax.rem(row, 2)
    z, xh = chip // 2, lax.rem(chip, 2)
    other = 2 * chip + 1 - core

    def chip_at(dz, dx):
        return lax.rem(z + dz, 4) * 2 + lax.rem(xh + dx, 2)

    steps = [(2, 1), (1, 1), (3, 1), (2, 0), (0, 1), (1, 0), (3, 0)]
    to_chips = [chip_at(dz, dx) for dz, dx in steps]
    from_chips = [chip_at(4 - dz, dx) for dz, dx in steps]
    xl, y = col // 4, lax.rem(col, 4)
    col_peers = [
        lax.rem(xl + dx, 2) * 4 + lax.rem(y + dy, 4) for dx, dy in [(1, 2), (1, 1), (1, 3), (0, 2), (1, 0), (0, 1), (0, 3)]
    ]
    n_chips = len(steps)

    load1 = pltpu.make_async_copy(b1_hbm, b1, load_sem.at[0])
    load2 = pltpu.make_async_copy(b2_hbm, b2, load_sem.at[1])
    load1.start()
    load2.start()
    barrier = pltpu.get_barrier_semaphore()
    for peer in to_chips:
        pl.semaphore_signal(barrier, inc=1, device_id=(2 * peer + core, col), device_id_type=MESH)
    for peer in col_peers:
        pl.semaphore_signal(barrier, inc=1, device_id=(row, peer), device_id_type=MESH)
    pl.semaphore_signal(barrier, inc=1, device_id=(other, col), device_id_type=MESH)
    for h in range(parts):
        x[h][pl.ds(OWN * row, OWN)] = vectors[:, h * height : (h + 1) * height, :]
    pl.semaphore_wait(barrier, n_chips + N_COL)

    def remote(src, dst, send, recv, device):
        return pltpu.make_async_remote_copy(
            src_ref=src, dst_ref=dst, send_sem=send, recv_sem=recv, device_id=device, device_id_type=MESH,
        )

    def unknowns(h, row):
        return x[h].at[pl.ds(OWN * row, OWN)]

    def gathers(h):
        return [
            remote(unknowns(h, row), unknowns(h, row), g_send.at[h, d], g_recv.at[h, d], (2 * peer + core, col))
            for d, peer in enumerate(to_chips)
        ]

    def relays(h, which=range(len(steps) + 1)):
        rows = [2 * peer + core for peer in from_chips] + [row]
        return [
            remote(unknowns(h, rows[d]), unknowns(h, rows[d]), y_send.at[h, d], y_recv.at[h, d], (other, col))
            for d in which
        ]

    def spreads(h):
        return [
            remote(part.at[h, peer], part_in.at[h, d], s_send.at[h, d], s_recv.at[h, d], (row, peer))
            for d, peer in enumerate(col_peers)
        ]

    def returns(h):
        mine = faces[h].at[pl.ds(FACES * col, FACES)]
        return [
            remote(mine, mine, a_send.at[h, d], a_recv.at[h, d], (row, peer)) for d, peer in enumerate(col_peers)
        ]

    def lends(h):
        return [remote(lent.at[h], lent_in.at[h], q_send.at[h], q_recv.at[h], (other, col))]

    def scatters(h):
        return [
            remote(middle.at[h, peer], middle_in.at[h, d], r_send.at[h, d], r_recv.at[h, d], (2 * peer + core, col))
            for d, peer in enumerate(to_chips)
        ]

    def start(copies):
        for copy in copies:
            copy.start()

    def arrived(copies):
        for copy in copies:
            copy.wait_recv()

    def left(copies):
        for copy in copies:
            copy.wait_send()

    def turn(n, values, turned):
        def body(step, carry):
            for u in range(8):
                turned[step * 8 + u] = values[step * 8 + u].T
            return carry

        lax.fori_loop(0, n // 8, body, 0)

    def sweep(which, n, values, source, sums):
        def body(step, total):
            products = []
            for u in range(UNROLL):
                at = step * UNROLL + u
                products.append(jnp.dot(
                    source[ints[3 * which + 1, at]], values[ints[3 * which, at]], preferred_element_type=F32
                ))
            for u in range(UNROLL):
                at = step * UNROLL + u
                total = total * floats[2 * which, at] + products[u]
                sums[at] = total
            return total

        if compute:
            lax.fori_loop(0, n // UNROLL, body, jnp.zeros((height, BLOCK), F32))

    def picked(which, sums, target):
        return sums[ints[3 * which + 2, target]] * floats[2 * which + 1, target]

    def forward(app, h):
        arrived(relays(h))
        if app == 0 and h == 0:
            load2.wait()
        sweep(FA, NB1, b1_turned, x[h], sums_a)
        sweep(FC, NB2, b2, x[h], sums_c)

        def hand_faces(m, carry):
            part[h, m, 0] = picked(FA, sums_a, m).astype(BF16)
            for b in range(FACES - 1):
                part[h, m, 1 + b] = picked(FC, sums_c, m * (FACES - 1) + b).astype(BF16)
            return carry

        lax.fori_loop(0, N_COL, hand_faces, 0)
        start(spreads(h))
        left(gathers(h) + relays(h))
        if app == 0 and h == 0:
            turn(NB2, b2, b2_turned)

    def sum_faces(app, h):
        arrived(spreads(h))

        def body(b, carry):
            total = part[h, col, b].astype(F32)
            for d in range(N_COL - 1):
                total = total + part_in[h, d, b].astype(F32)
            faces[h][col * FACES + b] = total.astype(BF16)
            return carry

        lax.fori_loop(0, FACES, body, 0)
        start(returns(h))

    def backward(app, h):
        arrived(returns(h))
        sweep(BA, NB1, b1, faces[h], sums_a)
        sweep(BC, NB2, b2_turned, faces[h], sums_c)

        def hand_image(m, carry):
            for b in range(OWN):
                t = (2 * m + 1 - core) * OWN + b
                lent[h, m, b] = (picked(BA, sums_a, t) + picked(BC, sums_c, t)).astype(BF16)
            return carry

        def keep_image(m, carry):
            for b in range(OWN):
                t = (2 * m + core) * OWN + b
                kept[h, m, b] = picked(BA, sums_a, t) + picked(BC, sums_c, t)
            return carry

        lax.fori_loop(0, N_ROW // 2, hand_image, 0)
        start(lends(h))
        lax.fori_loop(0, N_ROW // 2, keep_image, 0)
        left(spreads(h) + returns(h))

    def sum_cores(app, h):
        arrived(lends(h))

        def body(m, carry):
            for b in range(OWN):
                kept[h, m, b] = kept[h, m, b] + lent_in[h, m, b].astype(F32)
                middle[h, m, b] = kept[h, m, b].astype(BF16)
            return carry

        lax.fori_loop(0, N_ROW // 2, body, 0)
        start(scatters(h))

    def sum_chips(app, h):
        arrived(scatters(h))
        for b in range(OWN):
            total = kept[h, chip, b]
            for d in range(n_chips):
                total = total + middle_in[h, d, b].astype(F32)
            total = total * (1.0 / NORM)
            if app == apps - 1:
                out[b, h * height : (h + 1) * height, :] = total
            else:
                x[h][OWN * row + b] = total.astype(BF16)
        if app < apps - 1:
            begin(h)
        left(lends(h) + scatters(h))

    def begin(h):
        start(gathers(h) + relays(h, [n_chips]))

    def relay(app, h):
        for come, go in zip(gathers(h), relays(h, range(n_chips))):
            come.wait_recv()
            go.start()

    for h in range(parts):
        begin(h)
    load1.wait()
    turn(NB1, b1, b1_turned)
    run = {"Y": relay, "F": forward, "S": sum_faces, "B": backward, "Q": sum_cores, "R": sum_chips}
    for step, app, h in order or order_of(apps, parts):
        run[step](app, h)


def build(mesh, apps=APPS, parts=2, compute=True, order=None):
    tile = (K // parts, BLOCK)
    chips = N_ROW // 2

    def shards(vectors, b1_rows, b1_cols, b1_count, b1_values, b2_rows, b2_cols, b2_count, b2_values):
        counts = jnp.concatenate([b1_count[0], b2_count[0]])
        ints, floats = make_plans(counts, b1_rows[0], b1_cols[0], b2_rows[0], b2_cols[0])
        vmem = pl.BlockSpec(memory_space=pltpu.VMEM)
        smem = pl.BlockSpec(memory_space=pltpu.SMEM)
        hbm = pl.BlockSpec(memory_space=pl.ANY)
        dma = pltpu.SemaphoreType.DMA
        return pl.pallas_call(
            functools.partial(main_kernel, apps, parts, compute, order),
            out_shape=jax.ShapeDtypeStruct((OWN, K, BLOCK), F32),
            in_specs=[smem, smem, vmem, hbm, hbm],
            out_specs=vmem,
            scratch_shapes=[
                pltpu.VMEM((NB1, BLOCK, BLOCK), BF16),
                pltpu.VMEM((NB2, BLOCK, BLOCK), BF16),
                pltpu.VMEM((NB1, BLOCK, BLOCK), BF16),
                pltpu.VMEM((NB2, BLOCK, BLOCK), BF16),
                (pltpu.VMEM((EB_COL,) + tile, BF16),) * parts,
                pltpu.VMEM((NB2,) + tile, F32),
                pltpu.VMEM((NB1,) + tile, F32),
                pltpu.VMEM((parts, N_COL, FACES) + tile, BF16),
                pltpu.VMEM((parts, N_COL - 1, FACES) + tile, BF16),
                (pltpu.VMEM((N_COL * FACES,) + tile, BF16),) * parts,
                pltpu.VMEM((parts, chips, OWN) + tile, F32),
                pltpu.VMEM((parts, chips, OWN) + tile, BF16),
                pltpu.VMEM((parts, chips, OWN) + tile, BF16),
                pltpu.VMEM((parts, chips, OWN) + tile, BF16),
                pltpu.VMEM((parts, chips - 1, OWN) + tile, BF16),
                dma((2,)),
                dma((parts, chips - 1)), dma((parts, chips - 1)),
                dma((parts, chips)), dma((parts, chips)),
                dma((parts, N_COL - 1)), dma((parts, N_COL - 1)),
                dma((parts, N_COL - 1)), dma((parts, N_COL - 1)),
                dma((parts,)), dma((parts,)),
                dma((parts, chips - 1)), dma((parts, chips - 1)),
            ],
            compiler_params=pltpu.CompilerParams(
                collective_id=0, has_side_effects=True, vmem_limit_bytes=48 * 2**20
            ),
        )(ints, floats, vectors, b1_values[0, 0], b2_values[0, 0])

    return jax.shard_map(
        shards,
        mesh=mesh,
        in_specs=(
            P(("col", "row"), None, None),
            P("row", "col", None),
            P("row", "col", None),
            P("row", "col"),
            P("row", "col", None, None, None),
            P("row", "col", None),
            P("row", "col", None),
            P("row", "col"),
            P("row", "col", None, None, None),
        ),
        out_specs=P(("col", "row"), None, None),
        check_vma=False,
    )


def solution(mesh):
    return build(mesh)
```

time: 226 us -> 158 us (0.70)
  Pallas kernels: 219 us -> 149 us
    pallas_call x1, Pallas kernels: 216 us -> 147 us  [shards(): pl.pallas_call(functools.partial(main_kernel, apps, parts, compute, order...]
where the time goes in v2:
time: 158 us; the launch traced here: 155 us
  Pallas kernels  149 us (94%)
  local copies, waits for them, and re-layouts  4.03 us (3%)
    pallas_call x1, Pallas kernels, shards(): pl.pallas_call(functools.partial(main_kernel, apps, parts, compute, order...  147 us
    unnamed x9, local copies, waits for them, and re-layouts  4.03 us

profile of v2, /device:TPU:0, one launch (start us, length us, event | category | flops | bytes accessed | tf_op | source)
XLA Modules:
  0.0 154.9 jit_solution(1153436789426145226)
XLA Ops:
  1.3 0.6 pad_add_fusion.counts
  1.9 2.5 %shard_map.91 = (s32[12,256]{1,0:T(8,128)}, f32[8,256]{1,0:T(8,128)}) custom-call(s32[2]{0:T(128)} %pad_add_fusion.counts, s32[1,32]{1,0:T(1,128)} %bitcast.14, s32[1,32]{1,0:T(1,128)} %bitcast.15, s32[1,256]{1,0:T(1,128)} %bitcast.12, s32[1,256]{1,0:T(1,128)} %bitcast.13), custom_call_target="tpu_custom_call" | custom-call | tf_op jit(solution)/shard_map/pallas_call | solution.py:75
  4.3 0.0 copy-start
  4.4 1.2 copy-done
  5.6 0.0 copy-start.1
  5.6 0.8 copy-done.1
  6.3 0.0 copy-start.2
  6.3 0.7 copy-done.2
  7.1 0.0 copy-start.3
  7.1 0.7 copy-done.3
  7.7 146.5 %shard_map.92 = f32[2,64,128]{2,1,0:T(8,128)S(1)} custom-call(s32[12,256]{1,0:T(8,128)S(1)} %copy-done.2, f32[8,256]{1,0:T(8,128)S(1)} %copy-done.3, bf16[2,64,128]{2,1,0:T(8,128)(2,1)S(1)} %copy-done.1, bf16[32,128,128]{2,1,0:T(8,128)(2,1)S(1)} %bitcast.10, bf16[256,128,128]{2,1,0:T(8,128)(2,1)} %bitcast.11), custom_call_target="tpu_custom_call" | custom-call | tf_op jit(solution)/shard_map/pallas_call | solution.py:328
  154.3 0.6 copy.13
Async XLA Ops:
  4.3 1.2 copy-start
  5.6 0.8 copy-start.1
  6.3 0.7 copy-start.2
  7.1 0.7 copy-start.3

commit v3 on v2

--- a/solution.py
+++ b/solution.py
@@ -20,7 +20,7 @@
 N_COL = 8
 OWN = EB_COL // N_ROW
 FACES = 1 + TB_ROW // N_COL
-UNROLL = 32
+UNROLL = 64
 MESH = pl.DeviceIdType.MESH
 F32 = jnp.float32
 BF16 = jnp.bfloat16
@@ -28,7 +28,7 @@
 FC, FA, BC, BA = range(4)
 
 
-def plan_kernel(counts, b1_rows, b1_cols, b2_rows, b2_cols, ints, floats):
+def make_plans(count1, count2, rows1, cols1, rows2, cols2, ints, floats):
     def plan(which, target, source, filled, segments):
         n = target.shape[1]
         lanes = lax.broadcasted_iota(jnp.int32, (n, n), 1)
@@ -44,18 +44,17 @@
         hit = rank == lanes
         follows = (rank + 1) == lanes
 
-        def ordered(line, mask):
-            return jnp.sum(jnp.where(mask, column(line), 0), axis=0, keepdims=True)
-
-        here = ordered(target, hit)
-        before = ordered(target + 1, follows) - 1
-        slots = jnp.where(rank >= 0, rows, 0)
-        ints[3 * which : 3 * which + 1, :n] = jnp.sum(jnp.where(hit, slots, 0), axis=0, keepdims=True)
-        ints[3 * which + 1 : 3 * which + 2, :n] = ordered(source, hit)
+        def ordered(upright, mask):
+            return jnp.sum(jnp.where(mask, upright, 0), axis=0, keepdims=True)
+
+        upright = column(target)
+        here = ordered(upright, hit)
+        before = ordered(upright + 1, follows) - 1
+        ints[3 * which : 3 * which + 1, :n] = ordered(rows, hit)
+        ints[3 * which + 1 : 3 * which + 2, :n] = ordered(column(source), hit)
         floats[2 * which : 2 * which + 1, :n] = jnp.where(here == before, 1.0, 0.0)
         wide = 128
         segment = lax.broadcasted_iota(jnp.int32, (n, wide), 1)
-        upright = column(target)
         end = jnp.sum(jnp.where(upright <= segment, 1, 0), axis=0, keepdims=True)
         start = jnp.sum(jnp.where(upright < segment, 1, 0), axis=0, keepdims=True)
         ints[3 * which + 2 : 3 * which + 3, :wide] = jnp.maximum(end - 1, 0)
@@ -63,41 +62,17 @@
 
     ints[...] = jnp.zeros_like(ints)
     floats[...] = jnp.zeros_like(floats)
-    rows1, cols1, rows2, cols2 = b1_rows[...], b1_cols[...], b2_rows[...], b2_cols[...]
     per = TB_ROW // N_COL
-    plan(FC, cols2, rows2, counts[1], TB_ROW)
-    plan(FA, rows1, cols1, counts[0], VB_ROW)
-    plan(BC, rows2, (cols2 // per) * FACES + 1 + cols2 % per, counts[1], EB_COL)
-    plan(BA, cols1, rows1 * FACES, counts[0], EB_COL)
-
-
-def make_plans(counts, b1_rows, b1_cols, b2_rows, b2_cols):
-    return pl.pallas_call(
-        plan_kernel,
-        out_shape=(
-            jax.ShapeDtypeStruct((12, NB2), jnp.int32),
-            jax.ShapeDtypeStruct((8, NB2), F32),
-        ),
-        in_specs=[pl.BlockSpec(memory_space=pltpu.SMEM)] + [pl.BlockSpec(memory_space=pltpu.VMEM)] * 4,
-        out_specs=(pl.BlockSpec(memory_space=pltpu.VMEM),) * 2,
-    )(counts, b1_rows, b1_cols, b2_rows, b2_cols)
-
-
-def order_of(apps, parts):
-    if parts == 1:
-        return [(step, app, 0) for app in range(apps) for step in "YFSBQR"]
-    order = []
-    for app in range(apps):
-        order.append(("Y", app, 0))
-        if app:
-            order.append(("R", app - 1, 1))
-        order += [(step, app, h) for step, h in zip("FYFSSBQBRQ", (0, 1, 1, 0, 1, 0, 0, 1, 0, 1))]
-    return order + [("R", apps - 1, 1)]
+    plan(FC, cols2, rows2, count2, TB_ROW)
+    plan(FA, rows1, cols1, count1, VB_ROW)
+    plan(BC, rows2, (cols2 // per) * FACES + 1 + cols2 % per, count2, EB_COL)
+    plan(BA, cols1, rows1 * FACES, count1, EB_COL)
 
 
 def main_kernel(
-    apps, parts, compute, order,
-    ints, floats, vectors, b1_hbm, b2_hbm, out,
+    apps, parts, compute,
+    count1, count2, rows1_hbm, cols1_hbm, rows2_hbm, cols2_hbm, vectors, b1_hbm, b2_hbm, out,
+    rows1, cols1, rows2, cols2, ints_vector, floats_vector, ints, floats,
     b1, b2, b1_turned, b2_turned, x, sums_c, sums_a, part, part_in, faces,
     kept, lent, lent_in, middle, middle_in,
     load_sem, g_send, g_recv, y_send, y_recv, s_send, s_recv, a_send, a_recv, q_send, q_recv, r_send, r_recv,
@@ -120,18 +95,30 @@
     ]
     n_chips = len(steps)
 
-    load1 = pltpu.make_async_copy(b1_hbm, b1, load_sem.at[0])
-    load2 = pltpu.make_async_copy(b2_hbm, b2, load_sem.at[1])
-    load1.start()
-    load2.start()
+    def load(src, dst, at):
+        copy = pltpu.make_async_copy(src, dst, load_sem.at[at])
+        copy.start()
+        return copy
+
+    first = [
+        load(vectors.at[:, pl.ds(h * height, height), :], x[h].at[pl.ds(OWN * row, OWN)], h) for h in range(parts)
+    ]
+    lists = [
+        load(src, dst, parts + at)
+        for at, (src, dst) in enumerate(
+            [(rows1_hbm, rows1), (cols1_hbm, cols1), (rows2_hbm, rows2), (cols2_hbm, cols2)]
+        )
+    ]
+    load1 = load(b1_hbm, b1, parts + 4)
+    load2 = load(b2_hbm, b2, parts + 5)
     barrier = pltpu.get_barrier_semaphore()
     for peer in to_chips:
         pl.semaphore_signal(barrier, inc=1, device_id=(2 * peer + core, col), device_id_type=MESH)
     for peer in col_peers:
         pl.semaphore_signal(barrier, inc=1, device_id=(row, peer), device_id_type=MESH)
     pl.semaphore_signal(barrier, inc=1, device_id=(other, col), device_id_type=MESH)
-    for h in range(parts):
-        x[h][pl.ds(OWN * row, OWN)] = vectors[:, h * height : (h + 1) * height, :]
+    for copy in first:
+        copy.wait()
     pl.semaphore_wait(barrier, n_chips + N_COL)
 
     def remote(src, dst, send, recv, device):
@@ -197,29 +184,32 @@
         lax.fori_loop(0, n // 8, body, 0)
 
     def sweep(which, n, values, source, sums):
+        unroll = min(n, UNROLL)
+
         def body(step, total):
             products = []
-            for u in range(UNROLL):
-                at = step * UNROLL + u
-                products.append(jnp.dot(
-                    source[ints[3 * which + 1, at]], values[ints[3 * which, at]], preferred_element_type=F32
-                ))
-            for u in range(UNROLL):
-                at = step * UNROLL + u
+            for u in range(0, unroll, 2):
+                at = step * unroll + u
+                blocks = [values[ints[3 * which, at + i]] for i in range(2)]
+                picks = [source[ints[3 * which + 1, at + i]] for i in range(2)]
+                both = jnp.dot(
+                    jnp.concatenate(picks, axis=0), jnp.concatenate(blocks, axis=1), preferred_element_type=F32
+                )
+                products += [both[:height, :BLOCK], both[height:, BLOCK:]]
+            for u in range(unroll):
+                at = step * unroll + u
                 total = total * floats[2 * which, at] + products[u]
                 sums[at] = total
             return total
 
         if compute:
-            lax.fori_loop(0, n // UNROLL, body, jnp.zeros((height, BLOCK), F32))
+            lax.fori_loop(0, n // unroll, body, jnp.zeros((height, BLOCK), F32))
 
     def picked(which, sums, target):
         return sums[ints[3 * which + 2, target]] * floats[2 * which + 1, target]
 
     def forward(app, h):
         arrived(relays(h))
-        if app == 0 and h == 0:
-            load2.wait()
         sweep(FA, NB1, b1_turned, x[h], sums_a)
         sweep(FC, NB2, b2, x[h], sums_c)
 
@@ -232,8 +222,12 @@
         lax.fori_loop(0, N_COL, hand_faces, 0)
         start(spreads(h))
         left(gathers(h) + relays(h))
-        if app == 0 and h == 0:
-            turn(NB2, b2, b2_turned)
+
+        if h == 0:
+
+            @pl.when(app == 0)
+            def _():
+                turn(NB2, b2, b2_turned)
 
     def sum_faces(app, h):
         arrived(spreads(h))
@@ -289,12 +283,13 @@
             for d in range(n_chips):
                 total = total + middle_in[h, d, b].astype(F32)
             total = total * (1.0 / NORM)
-            if app == apps - 1:
-                out[b, h * height : (h + 1) * height, :] = total
-            else:
-                x[h][OWN * row + b] = total.astype(BF16)
-        if app < apps - 1:
+            out[b, h * height : (h + 1) * height, :] = total
+            x[h][OWN * row + b] = total.astype(BF16)
+
+        @pl.when(app < apps - 1)
+        def _():
             begin(h)
+
         left(lends(h) + scatters(h))
 
     def begin(h):
@@ -307,30 +302,63 @@
 
     for h in range(parts):
         begin(h)
+    for copy in lists:
+        copy.wait()
+    make_plans(count1[0, 0], count2[0, 0], rows1[...], cols1[...], rows2[...], cols2[...], ints_vector, floats_vector)
+    tables = [load(ints_vector, ints, parts + 6), load(floats_vector, floats, parts + 7)]
     load1.wait()
     turn(NB1, b1, b1_turned)
-    run = {"Y": relay, "F": forward, "S": sum_faces, "B": backward, "Q": sum_cores, "R": sum_chips}
-    for step, app, h in order or order_of(apps, parts):
-        run[step](app, h)
-
-
-def build(mesh, apps=APPS, parts=2, compute=True, order=None):
+    for copy in tables:
+        copy.wait()
+    load2.wait()
+    relay(0, 0)
+
+    def application(app, carry):
+        forward(app, 0)
+        for h in range(1, parts):
+            relay(app, h)
+            forward(app, h)
+        for h in range(parts):
+            sum_faces(app, h)
+        for h in range(parts):
+            backward(app, h)
+            sum_cores(app, h)
+            if h:
+                sum_chips(app, h - 1)
+
+        @pl.when(app < apps - 1)
+        def _():
+            relay(app + 1, 0)
+
+        sum_chips(app, parts - 1)
+        return carry
+
+    lax.fori_loop(0, apps, application, 0)
+
+
+def build(mesh, apps=APPS, parts=2, compute=True):
     tile = (K // parts, BLOCK)
     chips = N_ROW // 2
 
     def shards(vectors, b1_rows, b1_cols, b1_count, b1_values, b2_rows, b2_cols, b2_count, b2_values):
-        counts = jnp.concatenate([b1_count[0], b2_count[0]])
-        ints, floats = make_plans(counts, b1_rows[0], b1_cols[0], b2_rows[0], b2_cols[0])
         vmem = pl.BlockSpec(memory_space=pltpu.VMEM)
         smem = pl.BlockSpec(memory_space=pltpu.SMEM)
         hbm = pl.BlockSpec(memory_space=pl.ANY)
         dma = pltpu.SemaphoreType.DMA
         return pl.pallas_call(
-            functools.partial(main_kernel, apps, parts, compute, order),
+            functools.partial(main_kernel, apps, parts, compute),
             out_shape=jax.ShapeDtypeStruct((OWN, K, BLOCK), F32),
-            in_specs=[smem, smem, vmem, hbm, hbm],
+            in_specs=[smem] * 2 + [hbm] * 7,
             out_specs=vmem,
             scratch_shapes=[
+                pltpu.VMEM((1, NB1), jnp.int32),
+                pltpu.VMEM((1, NB1), jnp.int32),
+                pltpu.VMEM((1, NB2), jnp.int32),
+                pltpu.VMEM((1, NB2), jnp.int32),
+                pltpu.VMEM((16, NB2), jnp.int32),
+                pltpu.VMEM((8, NB2), F32),
+                pltpu.SMEM((16, NB2), jnp.int32),
+                pltpu.SMEM((8, NB2), F32),
                 pltpu.VMEM((NB1, BLOCK, BLOCK), BF16),
                 pltpu.VMEM((NB2, BLOCK, BLOCK), BF16),
                 pltpu.VMEM((NB1, BLOCK, BLOCK), BF16),
@@ -346,7 +374,7 @@
                 pltpu.VMEM((parts, chips, OWN) + tile, BF16),
                 pltpu.VMEM((parts, chips, OWN) + tile, BF16),
                 pltpu.VMEM((parts, chips - 1, OWN) + tile, BF16),
-                dma((2,)),
+                dma((parts + 8,)),
                 dma((parts, chips - 1)), dma((parts, chips - 1)),
                 dma((parts, chips)), dma((parts, chips)),
                 dma((parts, N_COL - 1)), dma((parts, N_COL - 1)),
@@ -355,9 +383,9 @@
                 dma((parts, chips - 1)), dma((parts, chips - 1)),
             ],
             compiler_params=pltpu.CompilerParams(
-                collective_id=0, has_side_effects=True, vmem_limit_bytes=48 * 2**20
+                collective_id=0, has_side_effects=True, vmem_limit_bytes=60 * 2**20
             ),
-        )(ints, floats, vectors, b1_values[0, 0], b2_values[0, 0])
+        )(b1_count, b2_count, b1_rows[0], b1_cols[0], b2_rows[0], b2_cols[0], vectors, b1_values[0, 0], b2_values[0, 0])
 
     return jax.shard_map(
         shards,

time: 158 us -> 141 us (0.89); the launches traced: 155 us -> 140 us
  Pallas kernels: 149 us -> 137 us
  local copies, waits for them, and re-layouts: 4.03 us -> 1.47 us
    pallas_call x2 -> x1, Pallas kernels: 149 us -> 137 us  [shards(): pl.pallas_call(functools.partial(main_kernel, apps, parts, compute), out_...]
    unnamed x9 -> x1, local copies, waits for them, and re-layouts: 4.03 us -> 1.47 us
where the time goes in v3:
time: 141 us; the launch traced here: 140 us
  Pallas kernels  137 us (97%)
  local copies, waits for them, and re-layouts  1.47 us (1%)
    pallas_call x1, Pallas kernels, shards(): pl.pallas_call(functools.partial(main_kernel, apps, parts, compute), out_...  137 us

profile of v3, /device:TPU:0, one launch (start us, length us, event | category | flops | bytes accessed | tf_op | source)
XLA Modules:
  0.0 140.3 jit_solution(11228477200281202864)
XLA Ops:
  1.3 137.5 %shard_map.91 = f32[2,64,128]{2,1,0:T(8,128)} custom-call(s32[1,1]{1,0:T(1,128)S(6)} %copy.11.count1, s32[1,1]{1,0:T(1,128)S(6)} %copy.12.count2, s32[1,32]{1,0:T(1,128)} %bitcast.10, s32[1,32]{1,0:T(1,128)} %bitcast.11, s32[1,256]{1,0:T(1,128)} %bitcast.8, s32[1,256]{1,0:T(1,128)} %bitcast.9, bf16[2,64,128]{2,1,0:T(8,128)(2,1)} %vectors.1, ...), custom_call_target="tpu_custom_call" | custom-call | tf_op jit(solution)/shard_map/pallas_call | solution.py:348
  138.8 1.5 %copy.13 = f32[2,64,128]{2,1,0:T(8,128)} copy(f32[2,64,128]{2,1,0:T(8,128)} %shard_map.91) | data formatting | bytes 131072

commit v4 on v3

--- a/solution.py
+++ b/solution.py
@@ -20,6 +20,10 @@
 N_COL = 8
 OWN = EB_COL // N_ROW
 FACES = 1 + TB_ROW // N_COL
+SIDES = 2
+RING = 4
+FIRST = 4
+SECOND = FACES - FIRST
 UNROLL = 64
 MESH = pl.DeviceIdType.MESH
 F32 = jnp.float32
@@ -63,19 +67,24 @@
     ints[...] = jnp.zeros_like(ints)
     floats[...] = jnp.zeros_like(floats)
     per = TB_ROW // N_COL
+
+    def face_place(member, block):
+        late = N_COL * FIRST + member * SECOND + block - FIRST
+        return jnp.where(block < FIRST, member * FIRST + block, late)
+
     plan(FC, cols2, rows2, count2, TB_ROW)
     plan(FA, rows1, cols1, count1, VB_ROW)
-    plan(BC, rows2, (cols2 // per) * FACES + 1 + cols2 % per, count2, EB_COL)
-    plan(BA, cols1, rows1 * FACES, count1, EB_COL)
+    plan(BC, rows2, face_place(cols2 // per, 1 + cols2 % per), count2, EB_COL)
+    plan(BA, cols1, rows1 * FIRST, count1, EB_COL)
 
 
 def main_kernel(
     apps, parts, compute,
     count1, count2, rows1_hbm, cols1_hbm, rows2_hbm, cols2_hbm, vectors, b1_hbm, b2_hbm, out,
     rows1, cols1, rows2, cols2, ints_vector, floats_vector, ints, floats,
-    b1, b2, b1_turned, b2_turned, x, sums_c, sums_a, part, part_in, faces,
+    b1, b2, b1_turned, b2_turned, x, sums_c, sums_a, part_p, part_q, p1_in, q1_in, mid_p, mid_q, own_q, p2_in, q2_in, faces,
     kept, lent, lent_in, middle, middle_in,
-    load_sem, g_send, g_recv, y_send, y_recv, s_send, s_recv, a_send, a_recv, q_send, q_recv, r_send, r_recv,
+    load_sem, g_send, g_recv, y_send, y_recv, c_send, c_recv, q_send, q_recv, r_send, r_recv,
 ):
     row, col = lax.axis_index("row"), lax.axis_index("col")
     height = K // parts
@@ -90,9 +99,9 @@
     to_chips = [chip_at(dz, dx) for dz, dx in steps]
     from_chips = [chip_at(4 - dz, dx) for dz, dx in steps]
     xl, y = col // 4, lax.rem(col, 4)
-    col_peers = [
-        lax.rem(xl + dx, 2) * 4 + lax.rem(y + dy, 4) for dx, dy in [(1, 2), (1, 1), (1, 3), (0, 2), (1, 0), (0, 1), (0, 3)]
-    ]
+    across = (row, (1 - xl) * RING + y)
+    ring_to = [lax.rem(y + dy, RING) for dy in (2, 1, 3)]
+    ring_from = [lax.rem(y + RING - dy, RING) for dy in (2, 1, 3)]
     n_chips = len(steps)
 
     def load(src, dst, at):
@@ -114,12 +123,12 @@
     barrier = pltpu.get_barrier_semaphore()
     for peer in to_chips:
         pl.semaphore_signal(barrier, inc=1, device_id=(2 * peer + core, col), device_id_type=MESH)
-    for peer in col_peers:
-        pl.semaphore_signal(barrier, inc=1, device_id=(row, peer), device_id_type=MESH)
+    for peer in [across] + [(row, xl * RING + to) for to in ring_to]:
+        pl.semaphore_signal(barrier, inc=1, device_id=peer, device_id_type=MESH)
     pl.semaphore_signal(barrier, inc=1, device_id=(other, col), device_id_type=MESH)
     for copy in first:
         copy.wait()
-    pl.semaphore_wait(barrier, n_chips + N_COL)
+    pl.semaphore_wait(barrier, n_chips + 1 + RING)
 
     def remote(src, dst, send, recv, device):
         return pltpu.make_async_remote_copy(
@@ -142,17 +151,51 @@
             for d in which
         ]
 
-    def spreads(h):
+    def hop(h, at, src, dst, device):
+        return remote(src, dst, c_send.at[h, at], c_recv.at[h, at], device)
+
+    def round_y(h, at, src_of, dst_of):
         return [
-            remote(part.at[h, peer], part_in.at[h, d], s_send.at[h, d], s_recv.at[h, d], (row, peer))
-            for d, peer in enumerate(col_peers)
+            hop(h, at + d, src_of(d, to), dst_of(d, to), (row, xl * RING + to)) for d, to in enumerate(ring_to)
         ]
 
-    def returns(h):
-        mine = faces[h].at[pl.ds(FACES * col, FACES)]
-        return [
-            remote(mine, mine, a_send.at[h, d], a_recv.at[h, d], (row, peer)) for d, peer in enumerate(col_peers)
-        ]
+    def firsts(h, start, count):
+        return faces[h].at[pl.ds(start * FIRST, count * FIRST)]
+
+    def seconds(h, member):
+        return faces[h].at[pl.ds(N_COL * FIRST + member * SECOND, SECOND)]
+
+    def across_p(h):
+        return [hop(h, 0, part_p.at[h, 1 - xl], p1_in.at[h], across)]
+
+    def around_q(h):
+        return round_y(h, 1, lambda d, to: part_q.at[h, :, to], lambda d, to: q1_in.at[h, d])
+
+    def around_p(h):
+        return round_y(h, 4, lambda d, to: mid_p.at[h, to], lambda d, to: p2_in.at[h, d])
+
+    def across_q(h):
+        return [hop(h, 7, mid_q.at[h], q2_in.at[h], across)]
+
+    def back_around_p(h):
+        mine = firsts(h, col, 1)
+        return round_y(h, 8, lambda d, to: mine, lambda d, to: mine)
+
+    def back_around_q(h):
+        mine = seconds(h, col)
+        return round_y(h, 11, lambda d, to: mine, lambda d, to: mine)
+
+    def back_across_q(h):
+        mine = seconds(h, col)
+        return [hop(h, 14, mine, mine, across)]
+
+    def back_across_p(h):
+        side = firsts(h, xl * RING, RING)
+        return [hop(h, 15, side, side, across)]
+
+    def back_around_again(h):
+        theirs = seconds(h, (1 - xl) * RING + y)
+        return round_y(h, 16, lambda d, to: theirs, lambda d, to: theirs)
 
     def lends(h):
         return [remote(lent.at[h], lent_in.at[h], q_send.at[h], q_recv.at[h], (other, col))]
@@ -214,36 +257,62 @@
         sweep(FC, NB2, b2, x[h], sums_c)
 
         def hand_faces(m, carry):
-            part[h, m, 0] = picked(FA, sums_a, m).astype(BF16)
-            for b in range(FACES - 1):
-                part[h, m, 1 + b] = picked(FC, sums_c, m * (FACES - 1) + b).astype(BF16)
+            side, at = m // RING, lax.rem(m, RING)
+            part_p[h, side, at, 0] = picked(FA, sums_a, m).astype(BF16)
+            for b in range(1, FIRST):
+                part_p[h, side, at, b] = picked(FC, sums_c, m * (FACES - 1) + b - 1).astype(BF16)
+            for b in range(SECOND):
+                part_q[h, side, at, b] = picked(FC, sums_c, m * (FACES - 1) + FIRST + b - 1).astype(BF16)
             return carry
 
         lax.fori_loop(0, N_COL, hand_faces, 0)
-        start(spreads(h))
+        start(across_p(h) + around_q(h))
         left(gathers(h) + relays(h))
 
-        if h == 0:
-
-            @pl.when(app == 0)
-            def _():
-                turn(NB2, b2, b2_turned)
+
+    def sum_pair(app, h):
+        arrived(across_p(h))
+
+        def body(to, carry):
+            for b in range(FIRST):
+                mid_p[h, to, b] = (part_p[h, xl, to, b].astype(F32) + p1_in[h, to, b].astype(F32)).astype(BF16)
+            return carry
+
+        lax.fori_loop(0, RING, body, 0)
+        start(around_p(h))
+
+    def sum_ring(app, h):
+        arrived(around_q(h))
+        for b in range(SECOND):
+            own = part_q[h, xl, y, b].astype(F32)
+            lent_sum = part_q[h, 1 - xl, y, b].astype(F32)
+            for d in range(RING - 1):
+                own = own + q1_in[h, d, xl, b].astype(F32)
+                lent_sum = lent_sum + q1_in[h, d, 1 - xl, b].astype(F32)
+            own_q[h, b] = own
+            mid_q[h, b] = lent_sum.astype(BF16)
+        start(across_q(h))
 
     def sum_faces(app, h):
-        arrived(spreads(h))
-
-        def body(b, carry):
-            total = part[h, col, b].astype(F32)
-            for d in range(N_COL - 1):
-                total = total + part_in[h, d, b].astype(F32)
-            faces[h][col * FACES + b] = total.astype(BF16)
-            return carry
-
-        lax.fori_loop(0, FACES, body, 0)
-        start(returns(h))
+        arrived(around_p(h) + across_q(h))
+        for b in range(SECOND):
+            faces[h][N_COL * FIRST + col * SECOND + b] = (own_q[h, b] + q2_in[h, b].astype(F32)).astype(BF16)
+        start(back_across_q(h))
+        for b in range(FIRST):
+            total = mid_p[h, y, b].astype(F32)
+            for d in range(RING - 1):
+                total = total + p2_in[h, d, b].astype(F32)
+            faces[h][col * FIRST + b] = total.astype(BF16)
+        start(back_around_p(h) + back_around_q(h))
+
+    def pass_on(app, h):
+        arrived(back_across_q(h))
+        start(back_around_again(h))
+        arrived(back_around_p(h))
+        start(back_across_p(h))
 
     def backward(app, h):
-        arrived(returns(h))
+        arrived(back_around_q(h) + back_around_again(h) + back_across_p(h))
         sweep(BA, NB1, b1, faces[h], sums_a)
         sweep(BC, NB2, b2_turned, faces[h], sums_c)
 
@@ -262,7 +331,8 @@
         lax.fori_loop(0, N_ROW // 2, hand_image, 0)
         start(lends(h))
         lax.fori_loop(0, N_ROW // 2, keep_image, 0)
-        left(spreads(h) + returns(h))
+        left(across_p(h) + around_q(h) + around_p(h) + across_q(h) + back_around_p(h) + back_around_q(h))
+        left(back_across_q(h) + back_across_p(h) + back_around_again(h))
 
     def sum_cores(app, h):
         arrived(lends(h))
@@ -308,18 +378,28 @@
     tables = [load(ints_vector, ints, parts + 6), load(floats_vector, floats, parts + 7)]
     load1.wait()
     turn(NB1, b1, b1_turned)
+    relay(0, 0)
     for copy in tables:
         copy.wait()
     load2.wait()
-    relay(0, 0)
 
     def application(app, carry):
         forward(app, 0)
         for h in range(1, parts):
             relay(app, h)
             forward(app, h)
+
+        @pl.when(app == 0)
+        def _():
+            turn(NB2, b2, b2_turned)
+
+        for h in range(parts):
+            sum_pair(app, h)
+            sum_ring(app, h)
         for h in range(parts):
             sum_faces(app, h)
+        for h in range(parts):
+            pass_on(app, h)
         for h in range(parts):
             backward(app, h)
             sum_cores(app, h)
@@ -366,8 +446,15 @@
                 (pltpu.VMEM((EB_COL,) + tile, BF16),) * parts,
                 pltpu.VMEM((NB2,) + tile, F32),
                 pltpu.VMEM((NB1,) + tile, F32),
-                pltpu.VMEM((parts, N_COL, FACES) + tile, BF16),
-                pltpu.VMEM((parts, N_COL - 1, FACES) + tile, BF16),
+                pltpu.VMEM((parts, SIDES, RING, FIRST) + tile, BF16),
+                pltpu.VMEM((parts, SIDES, RING, SECOND) + tile, BF16),
+                pltpu.VMEM((parts, RING, FIRST) + tile, BF16),
+                pltpu.VMEM((parts, RING - 1, SIDES, SECOND) + tile, BF16),
+                pltpu.VMEM((parts, RING, FIRST) + tile, BF16),
+                pltpu.VMEM((parts, SECOND) + tile, BF16),
+                pltpu.VMEM((parts, SECOND) + tile, F32),
+                pltpu.VMEM((parts, RING - 1, FIRST) + tile, BF16),
+                pltpu.VMEM((parts, SECOND) + tile, BF16),
                 (pltpu.VMEM((N_COL * FACES,) + tile, BF16),) * parts,
                 pltpu.VMEM((parts, chips, OWN) + tile, F32),
                 pltpu.VMEM((parts, chips, OWN) + tile, BF16),
@@ -377,8 +464,7 @@
                 dma((parts + 8,)),
                 dma((parts, chips - 1)), dma((parts, chips - 1)),
                 dma((parts, chips)), dma((parts, chips)),
-                dma((parts, N_COL - 1)), dma((parts, N_COL - 1)),
-                dma((parts, N_COL - 1)), dma((parts, N_COL - 1)),
+                dma((parts, 19)), dma((parts, 19)),
                 dma((parts,)), dma((parts,)),
                 dma((parts, chips - 1)), dma((parts, chips - 1)),
             ],

time: 141 us -> 135 us (0.957)
  Pallas kernels: 137 us -> 132 us
    pallas_call x1, Pallas kernels: 137 us -> 132 us  [shards(): pl.pallas_call(functools.partial(main_kernel, apps, parts, compute), out_...]
where the time goes in v4:
time: 135 us
  Pallas kernels  132 us (98%)
  local copies, waits for them, and re-layouts  1.47 us (1%)
    pallas_call x1, Pallas kernels, shards(): pl.pallas_call(functools.partial(main_kernel, apps, parts, compute), out_...  132 us

profile of v4, /device:TPU:0, one launch (start us, length us, event | category | flops | bytes accessed | tf_op | source)
XLA Modules:
  0.0 134.8 jit_solution(13531611387892475937)
XLA Ops:
  1.3 132.0 %shard_map.91 = f32[2,64,128]{2,1,0:T(8,128)} custom-call(s32[1,1]{1,0:T(1,128)S(6)} %copy.11.count1, s32[1,1]{1,0:T(1,128)S(6)} %copy.12.count2, s32[1,32]{1,0:T(1,128)} %bitcast.10, s32[1,32]{1,0:T(1,128)} %bitcast.11, s32[1,256]{1,0:T(1,128)} %bitcast.8, s32[1,256]{1,0:T(1,128)} %bitcast.9, bf16[2,64,128]{2,1,0:T(8,128)(2,1)} %vectors.1, ...), custom_call_target="tpu_custom_call" | custom-call | tf_op jit(solution)/shard_map/pallas_call | solution.py:428
  133.3 1.5 %copy.13 = f32[2,64,128]{2,1,0:T(8,128)} copy(f32[2,64,128]{2,1,0:T(8,128)} %shard_map.91) | data formatting | bytes 131072

commit v5 on v4

--- a/solution.py
+++ b/solution.py
@@ -24,7 +24,7 @@
 RING = 4
 FIRST = 4
 SECOND = FACES - FIRST
-UNROLL = 64
+UNROLL = 128
 MESH = pl.DeviceIdType.MESH
 F32 = jnp.float32
 BF16 = jnp.bfloat16
@@ -79,7 +79,7 @@
 
 
 def main_kernel(
-    apps, parts, compute,
+    apps, parts,
     count1, count2, rows1_hbm, cols1_hbm, rows2_hbm, cols2_hbm, vectors, b1_hbm, b2_hbm, out,
     rows1, cols1, rows2, cols2, ints_vector, floats_vector, ints, floats,
     b1, b2, b1_turned, b2_turned, x, sums_c, sums_a, part_p, part_q, p1_in, q1_in, mid_p, mid_q, own_q, p2_in, q2_in, faces,
@@ -245,7 +245,9 @@
                 sums[at] = total
             return total
 
-        if compute:
+        if n == unroll:
+            body(0, jnp.zeros((height, BLOCK), F32))
+        else:
             lax.fori_loop(0, n // unroll, body, jnp.zeros((height, BLOCK), F32))
 
     def picked(which, sums, target):
@@ -416,7 +418,7 @@
     lax.fori_loop(0, apps, application, 0)
 
 
-def build(mesh, apps=APPS, parts=2, compute=True):
+def build(mesh, apps=APPS, parts=2):
     tile = (K // parts, BLOCK)
     chips = N_ROW // 2
 
@@ -426,7 +428,7 @@
         hbm = pl.BlockSpec(memory_space=pl.ANY)
         dma = pltpu.SemaphoreType.DMA
         return pl.pallas_call(
-            functools.partial(main_kernel, apps, parts, compute),
+            functools.partial(main_kernel, apps, parts),
             out_shape=jax.ShapeDtypeStruct((OWN, K, BLOCK), F32),
             in_specs=[smem] * 2 + [hbm] * 7,
             out_specs=vmem,

time: 135 us -> 132 us (0.978)
  Pallas kernels: 132 us -> 129 us
    pallas_call x1, Pallas kernels: 132 us -> 129 us  [shards(): pl.pallas_call(functools.partial(main_kernel, apps, parts), out_shape=jax...]
where the time goes in v5:
time: 132 us
  Pallas kernels  129 us (98%)
  local copies, waits for them, and re-layouts  1.47 us (1%)
    pallas_call x1, Pallas kernels, shards(): pl.pallas_call(functools.partial(main_kernel, apps, parts), out_shape=jax...  129 us

profile of v5, /device:TPU:0, one launch (start us, length us, event | category | flops | bytes accessed | tf_op | source)
XLA Modules:
  0.0 131.9 jit_solution(17435476054293591612)
XLA Ops:
  1.3 129.1 %shard_map.91 = f32[2,64,128]{2,1,0:T(8,128)} custom-call(s32[1,1]{1,0:T(1,128)S(6)} %copy.11.count1, s32[1,1]{1,0:T(1,128)S(6)} %copy.12.count2, s32[1,32]{1,0:T(1,128)} %bitcast.10, s32[1,32]{1,0:T(1,128)} %bitcast.11, s32[1,256]{1,0:T(1,128)} %bitcast.8, s32[1,256]{1,0:T(1,128)} %bitcast.9, bf16[2,64,128]{2,1,0:T(8,128)(2,1)} %vectors.1, ...), custom_call_target="tpu_custom_call" | custom-call | tf_op jit(solution)/shard_map/pallas_call | solution.py:430
  130.4 1.5 %copy.13 = f32[2,64,128]{2,1,0:T(8,128)} copy(f32[2,64,128]{2,1,0:T(8,128)} %shard_map.91) | data formatting | bytes 131072

commit v6 on v5

--- a/solution.py
+++ b/solution.py
@@ -385,34 +385,49 @@
         copy.wait()
     load2.wait()
 
+    def faces_of(app, h, inner):
+        forward(app, h)
+        inner[0]()
+        sum_pair(app, h)
+        sum_ring(app, h)
+        inner[1]()
+        sum_faces(app, h)
+        pass_on(app, h)
+
+    def image_of(app, h):
+        backward(app, h)
+        sum_cores(app, h)
+
+    forward(0, 0)
+    turn(NB2, b2, b2_turned)
+    for step in (sum_pair, sum_ring, sum_faces, pass_on):
+        step(0, 0)
+    relay(0, 1)
+
     def application(app, carry):
-        forward(app, 0)
-        for h in range(1, parts):
-            relay(app, h)
-            forward(app, h)
-
-        @pl.when(app == 0)
-        def _():
-            turn(NB2, b2, b2_turned)
-
-        for h in range(parts):
-            sum_pair(app, h)
-            sum_ring(app, h)
-        for h in range(parts):
-            sum_faces(app, h)
-        for h in range(parts):
-            pass_on(app, h)
-        for h in range(parts):
-            backward(app, h)
-            sum_cores(app, h)
-            if h:
-                sum_chips(app, h - 1)
-
-        @pl.when(app < apps - 1)
+        more = pl.when(app < apps - 1)
+        faces_of(app, 1, (lambda: image_of(app, 0), lambda: sum_chips(app, 0)))
+
+        @more
         def _():
             relay(app + 1, 0)
-
-        sum_chips(app, parts - 1)
+            forward(app + 1, 0)
+
+        image_of(app, 1)
+
+        @more
+        def _():
+            sum_pair(app + 1, 0)
+            sum_ring(app + 1, 0)
+
+        sum_chips(app, 1)
+
+        @more
+        def _():
+            sum_faces(app + 1, 0)
+            pass_on(app + 1, 0)
+            relay(app + 1, 1)
+
         return carry
 
     lax.fori_loop(0, apps, application, 0)

time: 132 us -> 132 us (level); the launches traced: 132 us -> 130 us
  Pallas kernels: 129 us -> 127 us
    pallas_call x1, Pallas kernels: 129 us -> 127 us  [shards(): pl.pallas_call(functools.partial(main_kernel, apps, parts), out_shape=jax...]
where the time goes in v6:
time: 132 us; the launch traced here: 130 us
  Pallas kernels  127 us (96%)
  local copies, waits for them, and re-layouts  1.47 us (1%)
    pallas_call x1, Pallas kernels, shards(): pl.pallas_call(functools.partial(main_kernel, apps, parts), out_shape=jax...  127 us

profile of v6, /device:TPU:0, one launch (start us, length us, event | category | flops | bytes accessed | tf_op | source)
XLA Modules:
  0.0 130.1 jit_solution(17695802482272701289)
XLA Ops:
  1.3 127.3 %shard_map.91 = f32[2,64,128]{2,1,0:T(8,128)} custom-call(s32[1,1]{1,0:T(1,128)S(6)} %copy.11.count1, s32[1,1]{1,0:T(1,128)S(6)} %copy.12.count2, s32[1,32]{1,0:T(1,128)} %bitcast.10, s32[1,32]{1,0:T(1,128)} %bitcast.11, s32[1,256]{1,0:T(1,128)} %bitcast.8, s32[1,256]{1,0:T(1,128)} %bitcast.9, bf16[2,64,128]{2,1,0:T(8,128)(2,1)} %vectors.1, ...), custom_call_target="tpu_custom_call" | custom-call | tf_op jit(solution)/shard_map/pallas_call | solution.py:445
  128.6 1.5 %copy.13 = f32[2,64,128]{2,1,0:T(8,128)} copy(f32[2,64,128]{2,1,0:T(8,128)} %shard_map.91) | data formatting | bytes 131072
